TPU v7x, 32 devices: a whole 2x2x4 slice. The times are simulated.
32 devices in a mesh: groups: 2 (over y), replica: 4 (over z), tensor: 4 (over x, core).
Axes of the slice: x: 2, y: 2, z: 4, core: 2. Of those that a mesh axis runs over, the one named last changes fastest.
Arguments:
- queries: bfloat16 [8192, 8192], P(('groups', 'replica'), 'tensor'), parts along dimension 0, may hold values from -160 to 160
- suffix_cache: bfloat16 [8192, 2048], P(('groups', 'replica'), 'tensor'), parts along dimension 0, may hold values from -6 to 6
- cache_pool: bfloat16 [12288, 2048], P(('groups', 'replica'), 'tensor'), parts along dimension 0, may hold values from -6 to 6
- block_table: int32 [8, 4], P(('groups', 'replica')), parts along dimension 0, may hold values from 0 to 5, as said below
- prefix_blocks: int32 [8], P(('groups', 'replica')), parts along dimension 0, may hold values from 1 to 4, as said below
- segment_owner: int32 [128, 1], P(('groups', 'replica')), parts along dimension 0, may hold values from 0 to 3; in each aligned block of 16 rows (0 to 15, 16 to 31, ...) at most 8 rows name the same one
Outputs:
- placed_rows: bfloat16 [16384, 8192], P(('groups', 'replica'), 'tensor'), parts along dimension 0
There are 2 independent parts, one for each index of `groups`. A program takes and returns all parts, laid end to end along the dimension named above; each array names one. Nothing has to cross between parts.
Inputs may be any that keep to these rules, and one draw needn't show every extreme that they name: `block_table`: the 4 entries of a row are distinct. `prefix_blocks`: some request has exactly 4 blocks. `segment_owner`: among the segments of one request at most 8 share an owner, and some owner gets exactly 8.
All inputs are finite; a program needn't handle non-finite values.
Results may differ from a plain program's by a relative error of at most 0.0046.
Values may be sent and summed in bfloat16 or wider, within the bound.
No kernel may reach another device: no remote copies, remote signals or barrier semaphores. Data moves between devices by JAX's collectives and lax.ppermute only.
A program may use at most 192 MiB of HBM per device.

v0:
```python
import jax
import jax.numpy as jnp
from jax import lax
from jax.sharding import PartitionSpec as P

HEAD_DIM = 128
BLK = 256
MAXB = 4
POOL = 6
SEGS = 16
SEG = 64


def selection(owner_list, replicas, capacity):
    seg_order = jnp.arange(owner_list.shape[0], dtype=jnp.int32)
    same_owner = owner_list[None, :] == owner_list[:, None]
    earlier = seg_order[None, :] < seg_order[:, None]
    slot_index = jnp.sum((same_owner & earlier).astype(jnp.int32), axis=1)
    target = owner_list * capacity + slot_index
    return jnp.arange(replicas * capacity, dtype=jnp.int32)[:, None] == target[None, :]


def attend(queries, cache_rows, key_flags, query_pos, prefix_rows):
    query_count = queries.shape[0]
    key_count = cache_rows.shape[0]
    kv_heads = cache_rows.shape[1] // (2 * HEAD_DIM)
    group_size = queries.shape[1] // (HEAD_DIM * kv_heads)
    grouped = queries.reshape(query_count, kv_heads, group_size, HEAD_DIM)
    paired = cache_rows.reshape(key_count, kv_heads, 2, HEAD_DIM)
    scores = jnp.einsum(
        "qkgd,nkd->kgqn", grouped, paired[:, :, 0, :], preferred_element_type=jnp.float32
    ) * HEAD_DIM ** (-0.5)
    key_pos = jnp.arange(key_count, dtype=jnp.int32)
    allowed = jnp.where(
        key_pos[None, :] < prefix_rows,
        key_flags[None, :] > 0.5,
        key_pos[None, :] - prefix_rows <= query_pos[:, None],
    )
    highest = jnp.max(jnp.where(allowed, scores, -jnp.inf), axis=-1, keepdims=True)
    weights = jnp.exp(jnp.where(allowed, scores - highest, -jnp.inf))
    totals = jnp.sum(weights, axis=-1, keepdims=True)
    mixed = (
        jnp.einsum(
            "kgqn,nkd->kgqd",
            weights.astype(jnp.bfloat16),
            paired[:, :, 1, :],
            preferred_element_type=jnp.float32,
        )
        / totals
    )
    return jnp.transpose(mixed, (2, 0, 1, 3)).reshape(query_count, kv_heads * group_size * HEAD_DIM)


def body(queries, suffix_cache, cache_pool, block_table, prefix_blocks, segment_owner):
    replicas = lax.axis_size("replica")
    capacity = max(2, 2 * SEGS // replicas)
    prefix_rows = MAXB * BLK
    width = queries.shape[1]
    columns = cache_pool.shape[1]
    suffix_rows = queries.shape[0]
    seg_count = segment_owner.shape[0]
    home_pool = cache_pool.reshape(POOL, BLK, columns)
    prefix = jnp.take(home_pool, block_table[0], axis=0).reshape(prefix_rows, columns)
    cache_rows = jnp.concatenate([prefix, suffix_cache], axis=0)
    key_flags = jnp.concatenate(
        [
            (jnp.arange(prefix_rows, dtype=jnp.int32) < prefix_blocks[0] * BLK).astype(
                jnp.bfloat16
            ),
            jnp.ones((suffix_rows,), jnp.bfloat16),
        ]
    )
    chooser = selection(segment_owner[:, 0], replicas, capacity)
    chooser_mat = chooser.astype(jnp.bfloat16)
    own_rows = attend(
        queries, cache_rows, key_flags, jnp.arange(suffix_rows, dtype=jnp.int32), prefix_rows
    )
    own_rows = own_rows.astype(jnp.bfloat16)
    send_rows = jnp.dot(
        chooser_mat, own_rows.reshape(seg_count, SEG * width), preferred_element_type=jnp.float32
    ).astype(jnp.bfloat16)
    send_rows = send_rows.reshape(replicas, capacity * SEG, width)
    result = lax.all_to_all(send_rows, "replica", split_axis=0, concat_axis=0, tiled=True)
    return result.reshape(replicas * capacity * SEG, width)


def solution(mesh):
    in_specs = (
        P(("groups", "replica"), "tensor"),
        P(("groups", "replica"), "tensor"),
        P(("groups", "replica"), "tensor"),
        P(("groups", "replica"), None),
        P(("groups", "replica")),
        P(("groups", "replica"), None),
    )
    out_specs = P(("groups", "replica"), "tensor")
    return jax.shard_map(body, mesh=mesh, in_specs=in_specs, out_specs=out_specs, check_vma=False)
```

profile of v0, /device:TPU:0, one launch (start us, length us, event | category | flops | bytes accessed | tf_op | source)
XLA Modules:
  0.0 342.9 jit_solution(9908351910733243775)
XLA Ops:
  0.0 0.0 copy-start
  0.0 0.8 fusion.31
  0.8 0.7 compare_and_fusion
  2.1 0.0 copy-done
  2.1 0.6 gather_fusion
  2.8 1.2 gather.7
  4.0 0.1 broadcast_in_dim.54
  4.0 1.5 copy.16
  5.5 1.3 copy.17
  6.9 0.0 copy-start.1
  6.9 5.7 %copy.24 = bf16[128,8,16,128]{3,2,1,0:T(8,128)(2,1)} copy(bf16[128,8,16,128]{3,1,2,0:T(8,128)(2,1)} %bitcast.59) | data formatting | bytes 8388608
  12.6 0.0 copy-done.1
  12.6 0.0 copy-start.2
  12.6 1.2 copy_select_fusion
  13.8 3.6 %fusion.13 = pred[1024,2048]{0,1:T(8,128)(4,1)} fusion(s32[2048]{0:T(1024)S(1)} %iota_add_fusion, pred[2048]{0:T(1024)(128)(4,1)S(1)} %get-tuple-element.8, pred[2048]{0:T(1024)(128)(4,1)S(1)} %get-tuple-element.7), kind=kLoop, calls=%fused_computation.18 | loop fusion | flops 4194304 | bytes 2109440 | tf_op jit(solution)/shard_map/jit(_where)/select_n | solution.py:34
  17.3 0.0 copy-done.2
  17.3 59.9 %fusion.39 = (f32[2,8,1024]{2,1,0:T(8,128)S(1)}, bf16[2,8,1024,2048]{2,3,1,0:T(8,128)(2,1)}) fusion(pred[1024,2048]{0,1:T(8,128)(4,1)} %fusion.13, bf16[1024,2,8,128]{3,2,1,0:T(8,128)(2,1)} %bitcast.60, bf16[1024,2,2,128]{3,0,1,2:T(8,128)(2,1)} %copy_select_fusion, bf16[1024,2,2,128]{3,0,1,2:T(8,128)(2,1)S(1)} %copy-done.2), kind=kOutput, calls=%fused_computation.49 | convolution fusion | flops 17418946560 | bytes 83951616 | tf_op jit(solution)/shard_map/sub | solution.py:40
  77.3 36.4 %fusion.12 = bf16[1024,2,8,128]{3,0,2,1:T(8,128)(2,1)} fusion(f32[1024,2,8]{0,2,1:T(8,128)S(1)} %bitcast.63, bf16[2,8,1024,2048]{2,3,1,0:T(8,128)(2,1)} %get-tuple-element.6, bf16[1024,2,2,128]{3,0,1,2:T(8,128)(2,1)S(1)} %copy-done.2, bf16[1024,2,2,128]{3,0,1,2:T(8,128)(2,1)} %copy_select_fusion), kind=kOutput, calls=%fused_computation.16 | convolution fusion | flops 8596226048 | bytes 73465856 | tf_op jit(solution)/shard_map/kgqn,nkd->kgqd/dot_general | solution.py:43
  113.7 6.8 %copy.20 = bf16[1024,2,8,128]{3,2,1,0:T(8,128)(2,1)} copy(bf16[1024,2,8,128]{3,0,2,1:T(8,128)(2,1)} %fusion.12) | data formatting | bytes 8388608 | tf_op jit(solution)/shard_map/convert_element_type | solution.py:78
  120.5 0.0 copy-start.3
  120.5 4.7 %convert_element_type.21 = bf16[16,131072]{1,0:T(8,128)(2,1)} reshape(bf16[1024,2,8,128]{3,2,1,0:T(8,128)(2,1)} %copy.20) | data formatting | bytes 8388608 | tf_op jit(solution)/shard_map/convert_element_type | solution.py:78
  125.2 0.0 copy-done.3
  125.2 0.2 convert_reduce_fusion
  125.4 7.9 %convolution_convert_fusion = bf16[32,131072]{1,0:T(8,128)(2,1)} fusion(bf16[16,131072]{1,0:T(8,128)(2,1)} %convert_element_type.21, s32[16]{0:T(128)S(1)} %multiply_add_fusion), kind=kOutput, calls=%fused_computation.2 | convolution fusion | flops 138412544 | bytes 12582976 | tf_op jit(solution)/shard_map/dot_general | solution.py:79
  133.3 8.9 %reshape.89 = bf16[4,512,2048]{2,1,0:T(8,128)(2,1)} reshape(bf16[32,131072]{1,0:T(8,128)(2,1)} %convolution_convert_fusion) | data formatting | bytes 16777216 | tf_op jit(solution)/shard_map/reshape | solution.py:82
  142.2 192.2 %all_to_all.5 = bf16[4,512,2048]{2,1,0:T(8,128)(2,1)} all-to-all(bf16[4,512,2048]{2,1,0:T(8,128)(2,1)} %reshape.89), channel_id=1, replica_groups=mesh['groups'=2,'replica'=4,'tensor'=4] {'replica'}, dimensions={0} | all-to-all | bytes 16777216 | tf_op jit(solution)/shard_map/all_to_all | solution.py:83
  334.4 8.4 %copy.40 = bf16[2048,2048]{1,0:T(8,128)(2,1)} copy(bf16[2048,2048]{1,0:T(8,128)(2,1)} %bitcast.58) | data formatting | bytes 16777216
  (6 shorter events, 0.0 us)
Async XLA Ops:
  0.0 2.1 copy-start
  6.9 5.7 %copy-start.1 = (bf16[1024,2,2,128]{3,2,1,0:T(2,128)(2,1)S(1)}, bf16[1024,2,2,128]{3,2,1,0:T(2,128)(2,1)}, u32[]{:S(2)}) copy-start(bf16[1024,2,2,128]{3,2,1,0:T(2,128)(2,1)} %gather.7) | copy-start | bytes 3145732
  12.6 4.8 %copy-start.2 = (bf16[1024,2,2,128]{3,0,1,2:T(8,128)(2,1)S(1)}, bf16[1024,2,2,128]{3,0,1,2:T(8,128)(2,1)}, u32[]{:S(2)}) copy-start(bf16[1024,2,2,128]{3,0,1,2:T(8,128)(2,1)} %copy.17) | copy-start | bytes 3145732
  120.5 4.7 %copy-start.3 = (s32[16,1]{0,1:T(1,128)S(1)}, s32[16,1]{0,1:T(1,128)}, u32[]{:S(2)}) copy-start(s32[16,1]{0,1:T(1,128)} %param.11) | copy-start | bytes 196
where the time goes:
time: 343 us
  blocking collectives  192 us (56%)
  matrix products  104 us (30%)
  local copies, waits for them, and re-layouts  39.3 us (11%)
  other arithmetic  6.42 us (2%)
    all_to_all x1, blocking collectives, body(): lax.all_to_all(send_rows, 'replica', split_axis=0, concat_axis=0, tiled=T...  192 us
    sub x1, matrix products, attend(): weights = jnp.exp(jnp.where(allowed, scores - highest, -jnp.inf))  59.9 us
    dot_general x1, matrix products, attend(): jnp.einsum('kgqn,nkd->kgqd', weights.astype(jnp.bfloat16), paired[:, :, 1...  36.4 us
    unnamed x11, local copies, waits for them, and re-layouts  15.6 us
    convert_element_type x2, local copies, waits for them, and re-layouts, body(): own_rows = own_rows.astype(jnp.bfloat16)  11.5 us
    reshape x1, local copies, waits for them, and re-layouts, body(): send_rows = send_rows.reshape(replicas, capacity * SEG, width)  8.9 us
    dot_general x1, matrix products, body(): jnp.dot(chooser_mat, own_rows.reshape(seg_count, SEG * width), preferred_...  7.89 us

commit v1 on v0

v1 whole, which is shorter than its diff:
```python
import functools
import math

import jax
import jax.numpy as jnp
from jax import lax
from jax.experimental import pallas as pl
from jax.experimental.pallas import tpu as pltpu
from jax.sharding import PartitionSpec as P

HEAD_DIM = 128
BLK = 256
MAXB = 4
SEGS = 16
SEG = 64
EXPO = HEAD_DIM ** (-0.5) * math.log2(math.e)
LOWEST = -1e38


def attend_kernel(
    segs, table, blocks, q_ref, suffix_hbm, pool_hbm, o_ref, cache, scores, peak, acc, total, sems
):
    step = pl.program_id(0)
    seg = segs[step]
    suffix_rows = suffix_hbm.shape[0]
    kv_heads = suffix_hbm.shape[1] // (2 * HEAD_DIM)
    group = q_ref.shape[1] // (HEAD_DIM * kv_heads)
    rows = group * SEG

    @pl.when(step == 0)
    def _():
        copies = [
            pltpu.make_async_copy(suffix_hbm, cache.at[pl.ds(0, suffix_rows)], sems.at[MAXB])
        ]
        for b in range(MAXB):
            start = pl.multiple_of(table[b] * BLK, BLK)
            copies.append(
                pltpu.make_async_copy(
                    pool_hbm.at[pl.ds(start, BLK)],
                    cache.at[pl.ds(suffix_rows + b * BLK, BLK)],
                    sems.at[b],
                )
            )
        for copy in copies:
            copy.start()
        for copy in copies:
            copy.wait()

    @pl.when(seg < 0)
    def _():
        o_ref[...] = jnp.zeros_like(o_ref)

    @pl.when(seg >= 0)
    def _():
        whole = seg * SEG // BLK
        chunks = whole + blocks[0]

        def queries_of(g):
            first = g * group
            return jnp.concatenate(
                [q_ref[:, (first + h) * HEAD_DIM : (first + h + 1) * HEAD_DIM] for h in range(group)],
                axis=0,
            )

        def keys_of(start, g):
            return cache[pl.ds(start, BLK), 2 * g * HEAD_DIM : (2 * g + 1) * HEAD_DIM]

        def values_of(start, g):
            return cache[pl.ds(start, BLK), (2 * g + 1) * HEAD_DIM : (2 * g + 2) * HEAD_DIM]

        def start_of(t):
            start = jnp.where(t < whole, t * BLK, suffix_rows + (t - whole) * BLK)
            return pl.multiple_of(start, BLK)

        def dot_keys(start, g):
            return lax.dot_general(
                queries_of(g),
                keys_of(start, g),
                (((1,), (1,)), ((), ())),
                preferred_element_type=jnp.float32,
            )

        def halves_max(s):
            top = s[:, :HEAD_DIM]
            for c in range(1, BLK // HEAD_DIM):
                top = jnp.maximum(top, s[:, c * HEAD_DIM : (c + 1) * HEAD_DIM])
            return top

        last = pl.multiple_of(whole * BLK, BLK)
        token = lax.broadcasted_iota(jnp.int32, (rows, BLK), 0) % SEG + (seg * SEG - whole * BLK)
        seen = lax.broadcasted_iota(jnp.int32, (rows, BLK), 1) <= token
        for g in range(kv_heads):
            s = jnp.where(seen, dot_keys(last, g), LOWEST)
            scores[g, 0] = s
            peak[g] = halves_max(s)

        @pl.loop(0, chunks)
        def _(t):
            start = start_of(t)
            for g in range(kv_heads):
                s = dot_keys(start, g)
                scores[g, t + 1] = s
                peak[g] = jnp.maximum(peak[g], halves_max(s))

        for g in range(kv_heads):
            top = jnp.max(peak[g], axis=-1, keepdims=True)
            peak[g] = jnp.broadcast_to(top, (rows, HEAD_DIM))

        def weigh(start, t, g):
            top = peak[g]
            parts = [
                jnp.exp2((scores[g, t, :, c * HEAD_DIM : (c + 1) * HEAD_DIM] - top) * EXPO)
                for c in range(BLK // HEAD_DIM)
            ]
            mixed = jnp.dot(
                jnp.concatenate(parts, axis=1).astype(jnp.bfloat16),
                values_of(start, g),
                preferred_element_type=jnp.float32,
            )
            return mixed, sum(parts[1:], parts[0])

        for g in range(kv_heads):
            acc[g], total[g] = weigh(last, 0, g)

        @pl.loop(0, chunks)
        def _(t):
            start = start_of(t)
            for g in range(kv_heads):
                mixed, part = weigh(start, t + 1, g)
                acc[g] += mixed
                total[g] += part

        for g in range(kv_heads):
            out = (acc[g] / jnp.sum(total[g], axis=-1, keepdims=True)).astype(o_ref.dtype)
            for h in range(group):
                column = (g * group + h) * HEAD_DIM
                o_ref[:, column : column + HEAD_DIM] = out[h * SEG : (h + 1) * SEG]


def attend(segs, table, blocks, queries, suffix, pool):
    count = segs.shape[0]
    width = queries.shape[1]
    suffix_rows, columns = suffix.shape
    kv_heads = columns // (2 * HEAD_DIM)
    rows = width // (HEAD_DIM * kv_heads) * SEG
    keys = suffix_rows // 2 + MAXB * BLK
    chunks = suffix_rows // BLK + MAXB
    return pl.pallas_call(
        attend_kernel,
        out_shape=jax.ShapeDtypeStruct((count * SEG, width), queries.dtype),
        grid_spec=pltpu.PrefetchScalarGridSpec(
            num_scalar_prefetch=3,
            grid=(count,),
            in_specs=[
                pl.BlockSpec((SEG, width), lambda i, segs, *_: (jnp.maximum(segs[i], 0), 0)),
                pl.BlockSpec(memory_space=pl.ANY),
                pl.BlockSpec(memory_space=pl.ANY),
            ],
            out_specs=pl.BlockSpec((SEG, width), lambda i, *_: (i, 0)),
            scratch_shapes=[
                pltpu.VMEM((suffix_rows + MAXB * BLK, columns), suffix.dtype),
                pltpu.VMEM((kv_heads, chunks, rows, BLK), jnp.float32),
                pltpu.VMEM((kv_heads, rows, HEAD_DIM), jnp.float32),
                pltpu.VMEM((kv_heads, rows, HEAD_DIM), jnp.float32),
                pltpu.VMEM((kv_heads, rows, HEAD_DIM), jnp.float32),
                pltpu.SemaphoreType.DMA((MAXB + 1,)),
            ],
        ),
        compiler_params=pltpu.CompilerParams(vmem_limit_bytes=40 * 2**20),
        cost_estimate=pl.CostEstimate(
            flops=8 * count * SEG * width * keys,
            bytes_accessed=2 * (2 * count * SEG * width + 2 * suffix_rows * columns),
            transcendentals=count * SEG * keys * width // HEAD_DIM,
        ),
    )(segs, table, blocks, queries, suffix, pool)


def place_kernel(spans, starts, *refs):
    pieces, out, sems = refs[: len(spans)], refs[len(spans)], refs[len(spans) + 1]
    copies = []
    for i, rows in enumerate(spans):
        start = pl.multiple_of(starts[i], SEG)
        copies.append(pltpu.make_async_copy(pieces[i], out.at[pl.ds(start, rows)], sems.at[i]))
    for copy in copies:
        copy.start()
    for copy in copies:
        copy.wait()


def place(pieces, starts, rows):
    spans = [piece.shape[0] for piece in pieces]
    assert sum(spans) == rows
    return pl.pallas_call(
        functools.partial(place_kernel, spans),
        out_shape=jax.ShapeDtypeStruct((rows, pieces[0].shape[1]), pieces[0].dtype),
        grid_spec=pltpu.PrefetchScalarGridSpec(
            num_scalar_prefetch=1,
            grid=(),
            in_specs=[pl.BlockSpec(memory_space=pl.ANY)] * len(pieces),
            out_specs=pl.BlockSpec(memory_space=pl.ANY),
            scratch_shapes=[pltpu.SemaphoreType.DMA((len(pieces),))],
        ),
        cost_estimate=pl.CostEstimate(
            flops=0, bytes_accessed=4 * rows * pieces[0].shape[1], transcendentals=0
        ),
    )(starts, *pieces)


def swap(rows, distance):
    size = lax.axis_size("replica")
    return lax.ppermute(rows, "replica", [(i, i ^ distance) for i in range(size)])


def swap_some(rows, distance, segments):
    def branch(count):
        def run(rows):
            if count == 0:
                return jnp.zeros_like(rows)
            got = swap(rows[: count * SEG], distance)
            return jnp.pad(got, ((0, rows.shape[0] - got.shape[0]), (0, 0)))

        return run

    return lax.switch(segments, [branch(c) for c in range(rows.shape[0] // SEG + 1)], rows)


def body(queries, suffix_cache, cache_pool, block_table, prefix_blocks, segment_owner):
    replicas = lax.axis_size("replica")
    me = lax.axis_index("replica")
    capacity = max(2, 2 * SEGS // replicas)
    base = SEGS // replicas
    order = jnp.arange(SEGS, dtype=jnp.int32)
    owner = segment_owner[:, 0]
    same = owner[None, :] == owner[:, None]
    slot = jnp.sum((same & (order[None, :] < order[:, None])).astype(jnp.int32), axis=1)
    distance = owner ^ me
    chooser = (distance[None, None, :] == jnp.arange(replicas, dtype=jnp.int32)[:, None, None]) & (
        slot[None, None, :] == jnp.arange(capacity, dtype=jnp.int32)[None, :, None]
    )
    segs = jnp.sum(jnp.where(chooser, order + 1, 0), axis=2) - 1
    counts = jnp.sum((segs >= 0).astype(jnp.int32), axis=1)
    every = lax.all_gather(counts, "replica")
    others = jnp.arange(replicas, dtype=jnp.int32)
    incoming = jnp.sum(
        jnp.where(others[:, None] ^ me == others[None, :], every, 0), axis=0
    )
    extra = jnp.clip(jnp.maximum(counts, incoming) - base, 0, capacity - base)

    run = lambda ids: attend(
        ids, block_table[0], prefix_blocks, queries, suffix_cache, cache_pool
    )
    far = list(range(replicas - 1, 0, -1))
    if replicas == 4:
        stages = [[(3, 0, 2)], [(2, 0, 2)], [(3, 2, 4)], [(2, 2, 4)], [(1, 0, 4)]]
    else:
        stages = [[(k, 0, base) for k in far]]
    pieces, starts = [], []

    def put(rows, k, first):
        pieces.append(rows)
        starts.append(((me ^ k) * capacity + first) * SEG)

    for stage in stages:
        rows = run(jnp.concatenate([segs[k, a:b] for k, a, b in stage]))
        at = 0
        for k, a, b in stage:
            put(swap(rows[at : at + (b - a) * SEG], k), k, a)
            at += (b - a) * SEG
    rest = run(jnp.concatenate([segs[k, base:] for k in far] + [segs[0]]))
    span = (capacity - base) * SEG
    for i, k in enumerate(far):
        put(swap_some(rest[i * span : (i + 1) * span], k, extra[k]), k, base)
    put(rest[len(far) * span :], 0, 0)
    return place(pieces, jnp.stack(starts).astype(jnp.int32), replicas * capacity * SEG)


def solution(mesh):
    in_specs = (
        P(("groups", "replica"), "tensor"),
        P(("groups", "replica"), "tensor"),
        P(("groups", "replica"), "tensor"),
        P(("groups", "replica"), None),
        P(("groups", "replica")),
        P(("groups", "replica"), None),
    )
    out_specs = P(("groups", "replica"), "tensor")
    return jax.shard_map(body, mesh=mesh, in_specs=in_specs, out_specs=out_specs, check_vma=False)
```

time: 343 us -> 463 us (1.35)
  the two profiles are of different devices: /device:TPU:0 before, /device:TPU:24 now
where the time goes in v1:
time: 463 us; the launch traced here: 459 us
  Pallas kernels  340 us (73%)
  blocking collectives  35.5 us (8%)
  starting transfers between devices  34.1 us (7%)
  waiting for transfers between devices  22.9 us (5%)
  local copies, waits for them, and re-layouts  21.3 us (5%)
    pallas_call x1, Pallas kernels, place(): pl.pallas_call(functools.partial(place_kernel, spans), out_shape=jax.Shap...  256 us
    pallas_call x6, Pallas kernels, attend(): pl.pallas_call(attend_kernel, out_shape=jax.ShapeDtypeStruct((count * SEG...  83.7 us
    unnamed x1, blocking collectives  35.5 us
    ppermute x6, starting transfers between devices, swap(): lax.ppermute(rows, 'replica', [(i, i ^ distance) for i in range(size)])  34.1 us
    ppermute x6, waiting for transfers between devices, swap(): lax.ppermute(rows, 'replica', [(i, i ^ distance) for i in range(size)])  22.9 us
    unnamed x31, local copies, waits for them, and re-layouts  12.3 us
  transfers between devices with their start and end apart: 6, of which 2 were waited for; matrix products, arithmetic and copies ran while one was open for 2% of the time, Pallas kernels for 17%

profile of v1, /device:TPU:24, one launch (start us, length us, event | category | flops | bytes accessed | tf_op | source)
XLA Modules:
  0.0 458.9 jit_solution(411759031180336383)
XLA Ops:
  0.7 0.9 convert_reduce_fusion
  1.6 0.7 broadcast_xor_fusion
  2.2 0.2 select_reduce_fusion
  2.4 0.1 convert_reduce_fusion.1
  2.5 0.1 slice_bitcast_fusion.5
  2.6 2.2 copy-done
  4.8 1.4 copy-done.4
  6.2 1.2 copy-done.6
  7.4 0.7 copy-done.10
  8.1 7.7 %shard_map.64 = bf16[128,2048]{1,0:T(8,128)(2,1)S(1)} custom-call(s32[2]{0:T(128)S(1)} %get-tuple-element.56.segs, s32[4]{0:T(128)S(1)} %bitcast.34, s32[1]{0:T(128)S(6)} %copy.23.blocks, bf16[1024,2048]{1,0:T(8,128)(2,1)S(1)} %copy-done, bf16[1024,512]{1,0:T(8,128)(2,1)S(1)} %copy-done.6, bf16[1536,512]{1,0:T(8,128)(2,1)S(1)} %copy-done.4), custom_call_target="tpu_custom_call" | custom-call | flops 3221225472 | bytes 3145728 | tf_op jit(solution)/shard_map/pallas_call | solution.py:148
  15.8 0.1 collective-permute-start.12
  15.8 10.9 %shard_map.65 = bf16[128,2048]{1,0:T(8,128)(2,1)} custom-call(s32[2]{0:T(128)S(1)} %get-tuple-element.55.segs, s32[4]{0:T(128)S(1)} %bitcast.35, s32[1]{0:T(128)S(6)} %copy.23.blocks, bf16[1024,2048]{1,0:T(8,128)(2,1)S(1)} %copy-done.1, bf16[1024,512]{1,0:T(8,128)(2,1)S(1)} %copy-done.6, bf16[1536,512]{1,0:T(8,128)(2,1)S(1)} %copy-done.4), custom_call_target="tpu_custom_call" | custom-call | flops 3221225472 | bytes 3145728 | tf_op jit(solution)/shard_map/pallas_call | solution.py:148
  26.8 0.7 collective-permute-start.13
  27.4 9.0 %shard_map.66 = bf16[128,2048]{1,0:T(8,128)(2,1)} custom-call(s32[2]{0:T(128)S(1)} %get-tuple-element.54.segs, s32[4]{0:T(128)S(1)} %bitcast.36, s32[1]{0:T(128)S(6)} %copy.23.blocks, bf16[1024,2048]{1,0:T(8,128)(2,1)S(1)} %copy-done.1, bf16[1024,512]{1,0:T(8,128)(2,1)S(1)} %copy-done.6, bf16[1536,512]{1,0:T(8,128)(2,1)S(1)} %copy-done.4), custom_call_target="tpu_custom_call" | custom-call | flops 3221225472 | bytes 3145728 | tf_op jit(solution)/shard_map/pallas_call | solution.py:148
  36.4 4.0 collective-permute-start.14
  40.4 0.1 slice_bitcast_fusion.3
  40.5 19.7 %shard_map.68 = bf16[256,2048]{1,0:T(8,128)(2,1)} custom-call(s32[4]{0:T(128)S(1)} %get-tuple-element.50.segs, s32[4]{0:T(128)S(1)} %bitcast.37, s32[1]{0:T(128)S(6)} %copy.23.blocks, bf16[1024,2048]{1,0:T(8,128)(2,1)S(1)} %copy-done.1, bf16[1024,512]{1,0:T(8,128)(2,1)S(1)} %copy-done.6, bf16[1536,512]{1,0:T(8,128)(2,1)S(1)} %copy-done.5), custom_call_target="tpu_custom_call" | custom-call | flops 6442450944 | bytes 4194304 | tf_op jit(solution)/shard_map/pallas_call | solution.py:148
  60.2 0.1 collective-permute-start.16
  60.4 0.6 dynamic-slice
  61.6 0.2 dynamic-update-slice
  61.8 35.5 %all-reduce.9 = s32[16]{0:T(128)S(1)} all-reduce(s32[16]{0:T(128)S(1)} %dynamic-update-slice), channel_id=2, replica_groups=mesh['groups'=2,'replica'=4,'tensor'=4] {'replica'}, use_global_device_ids=true, to_apply=%add.9 | all-reduce | flops 16 | bytes 128
  97.3 0.1 reshape.67
  97.4 0.1 pad_add_fusion.segs
  97.5 2.2 copy-done.2
  99.7 24.9 %shard_map.69 = bf16[1280,2048]{1,0:T(8,128)(2,1)} custom-call(s32[20]{0:T(128)S(1)} %pad_add_fusion.segs, s32[4]{0:T(128)S(1)} %bitcast.38, s32[1]{0:T(128)S(6)} %copy.23.blocks, bf16[1024,2048]{1,0:T(8,128)(2,1)S(1)} %copy-done.2, bf16[1024,512]{1,0:T(8,128)(2,1)S(1)} %copy-done.7, bf16[1536,512]{1,0:T(8,128)(2,1)S(1)} %copy-done.5), custom_call_target="tpu_custom_call" | custom-call | flops 32212254720 | bytes 12582912 | tf_op jit(solution)/shard_map/pallas_call | solution.py:148
  124.6 0.1 select_reduce_fusion.1
  124.7 0.7 fusion.1
  127.3 1.1 conditional.5
  127.3 1.1 broadcast.67
  128.4 2.2 copy-done.3
  130.6 11.5 %shard_map.67 = bf16[128,2048]{1,0:T(8,128)(2,1)S(1)} custom-call(s32[2]{0:T(128)S(1)} %get-tuple-element.53.segs, s32[4]{0:T(128)S(1)} %bitcast.39, s32[1]{0:T(128)S(6)} %copy.23.blocks, bf16[1024,2048]{1,0:T(8,128)(2,1)S(1)} %copy-done.3, bf16[1024,512]{1,0:T(8,128)(2,1)S(1)} %copy-done.7, bf16[1536,512]{1,0:T(8,128)(2,1)S(1)} %copy-done.5), custom_call_target="tpu_custom_call" | custom-call | flops 3221225472 | bytes 3145728 | tf_op jit(solution)/shard_map/pallas_call | solution.py:148
  142.1 0.8 copy-done.8
  142.9 46.4 %conditional.4 = (bf16[256,2048]{1,0:T(8,128)(2,1)}) conditional(s32[]{:T(128)} %bitcast.22, () %tuple.51, bf16[1280,2048]{1,0:T(8,128)(2,1)} %shard_map.69, bf16[1280,2048]{1,0:T(8,128)(2,1)} %shard_map.69, bf16[1280,2048]{1,0:T(8,128)(2,1)} %shard_map.69, bf16[1280,2048]{1,0:T(8,128)(2,1)} %shard_map.69), branch_computations={%region_9.10_spmd, %region_10.11_spmd, %region_11.12_spmd, %region... | conditional | bytes 6553650 | solution.py:224
  142.9 1.0 slice.99
  143.8 29.3 %collective-permute-start.4 = (bf16[64,2048]{1,0:T(8,128)(2,1)S(1)}, bf16[64,2048]{1,0:T(8,128)(2,1)S(1)}, u32[]{:S(2)}, u32[]{:S(2)}) collective-permute-start(bf16[64,2048]{1,0:T(8,128)(2,1)S(1)} %slice.99), channel_id=1, source_target_pairs={{0,8},{4,12},{8,0},{12,4},{1,9},{5,13},{9,1},{13,5},{2,10},{6,14},... | collective-permute-start | bytes 786440 | tf_op jit(solution)/shard_map/cond/branch_1_fun/ppermute | solution.py:211
  173.2 15.0 %collective-permute-done.4 = bf16[64,2048]{1,0:T(8,128)(2,1)S(1)} collective-permute-done((bf16[64,2048]{1,0:T(8,128)(2,1)S(1)}, bf16[64,2048]{1,0:T(8,128)(2,1)S(1)}, u32[]{:S(2)}, u32[]{:S(2)}) %collective-permute-start.4) | collective-permute-done | bytes 262176 | tf_op jit(solution)/shard_map/cond/branch_1_fun/ppermute | solution.py:211
  188.2 1.1 pad.24
  189.3 1.1 conditional.3
  189.3 1.1 broadcast.53
  190.4 0.0 collective-permute-start.15
  190.4 3.2 slice.133.refs_8_
  193.6 0.7 stack.39.starts
  194.2 0.0 collective-permute-done.12.refs_0_
  194.2 0.0 collective-permute-done.13.refs_1_
  194.2 0.0 collective-permute-done.14.refs_2_
  194.3 7.9 %collective-permute-done.15.refs_3_ = bf16[128,2048]{1,0:T(8,128)(2,1)S(1)} collective-permute-done((bf16[128,2048]{1,0:T(8,128)(2,1)S(1)}, bf16[128,2048]{1,0:T(8,128)(2,1)S(1)}, u32[]{:S(2)}, u32[]{:S(2)}) %collective-permute-start.15) | collective-permute-done | bytes 524320 | tf_op jit(solution)/shard_map/ppermute | solution.py:211
  202.1 0.8 copy-done.12
  202.9 256.0 %shard_map.70 = bf16[2048,2048]{1,0:T(8,128)(2,1)} custom-call(s32[9]{0:T(128)} %stack.39.starts, bf16[128,2048]{1,0:T(8,128)(2,1)} %collective-permute-done.12.refs_0_, bf16[128,2048]{1,0:T(8,128)(2,1)} %collective-permute-done.13.refs_1_, bf16[128,2048]{1,0:T(8,128)(2,1)} %collective-permute-done.14.refs_2_, bf16[128,2048]{1,0:T(8,128)(2,1)} %copy-done.12, ...), custom_call_target="tpu_custom_call" | custom-call | bytes 16777216 | tf_op jit(solution)/shard_map/pallas_call | solution.py:193
  (28 shorter events, 0.1 us)
Async XLA Ops:
  2.6 2.2 copy-start
  4.8 1.4 copy-start.4
  6.2 1.2 copy-start.6
  7.4 0.7 copy-start.10
  8.1 7.8 %copy-start.1 = (bf16[1024,2048]{1,0:T(8,128)(2,1)S(1)}, bf16[1024,2048]{1,0:T(8,128)(2,1)}, u32[]{:S(2)}) copy-start(bf16[1024,2048]{1,0:T(8,128)(2,1)} %q_ref.11) | copy-start | bytes 12582916
  15.8 178.5 %collective-permute-start.12 = (bf16[128,2048]{1,0:T(8,128)(2,1)S(1)}, bf16[128,2048]{1,0:T(8,128)(2,1)}, u32[]{:S(2)}, u32[]{:S(2)}) collective-permute-start(bf16[128,2048]{1,0:T(8,128)(2,1)S(1)} %shard_map.64), channel_id=1, source_target_pairs={{0,12},{4,8},{8,4},{12,0},{1,13},{5,9},{9,5},{13,1},{2,14},{6,10},... | collective-permute-start | bytes 1572872 | tf_op jit(solution)/shard_map/ppermute | solution.py:211
  26.8 167.5 %collective-permute-start.13 = (bf16[128,2048]{1,0:T(8,128)(2,1)}, bf16[128,2048]{1,0:T(8,128)(2,1)}, u32[]{:S(2)}, u32[]{:S(2)}) collective-permute-start(bf16[128,2048]{1,0:T(8,128)(2,1)} %shard_map.65), channel_id=1, source_target_pairs={{0,8},{4,12},{8,0},{12,4},{1,9},{5,13},{9,1},{13,5},{2,10},{6,14},... | collective-permute-start | bytes 1572872 | tf_op jit(solution)/shard_map/ppermute | solution.py:211
  27.4 13.1 %copy-start.5 = (bf16[1536,512]{1,0:T(8,128)(2,1)S(1)}, bf16[1536,512]{1,0:T(8,128)(2,1)}, u32[]{:S(2)}) copy-start(bf16[1536,512]{1,0:T(8,128)(2,1)} %pool_hbm.11) | copy-start | bytes 4718596
  36.4 157.8 %collective-permute-start.14 = (bf16[128,2048]{1,0:T(8,128)(2,1)}, bf16[128,2048]{1,0:T(8,128)(2,1)}, u32[]{:S(2)}, u32[]{:S(2)}) collective-permute-start(bf16[128,2048]{1,0:T(8,128)(2,1)} %shard_map.66), channel_id=1, source_target_pairs={{0,12},{4,8},{8,4},{12,0},{1,13},{5,9},{9,5},{13,1},{2,14},{6,10},... | collective-permute-start | bytes 1572872 | tf_op jit(solution)/shard_map/ppermute | solution.py:211
  40.5 19.9 %copy-start.13 = (u32[32]{0:T(128)S(1)}, u32[32]{0:T(128)}, u32[]{:S(2)}) copy-start(u32[32]{0:T(128)} %constant.98) | copy-start | bytes 388
  40.5 57.0 %copy-start.7 = (bf16[1024,512]{1,0:T(8,128)(2,1)S(1)}, bf16[1024,512]{1,0:T(8,128)(2,1)}, u32[]{:S(2)}) copy-start(bf16[1024,512]{1,0:T(8,128)(2,1)} %suffix_hbm.11) | copy-start | bytes 3145732
  40.5 57.0 %copy-start.11 = (s32[1,4]{1,0:T(1,128)S(1)}, s32[1,4]{1,0:T(1,128)}, u32[]{:S(2)}) copy-start(s32[1,4]{1,0:T(1,128)} %param.24) | copy-start | bytes 52
  60.2 141.9 %collective-permute-start.16 = (bf16[256,2048]{1,0:T(8,128)(2,1)}, bf16[256,2048]{1,0:T(8,128)(2,1)}, u32[]{:S(2)}, u32[]{:S(2)}) collective-permute-start(bf16[256,2048]{1,0:T(8,128)(2,1)} %shard_map.68), channel_id=1, source_target_pairs={{0,4},{4,0},{8,12},{12,8},{1,5},{5,1},{9,13},{13,9},{2,6},{6,2},{1... | collective-permute-start | bytes 3145736 | tf_op jit(solution)/shard_map/ppermute | solution.py:211
  97.5 2.2 copy-start.2
  128.4 2.2 copy-start.3
  142.1 0.8 copy-start.8
  143.8 44.3 %collective-permute-start.4 = (bf16[64,2048]{1,0:T(8,128)(2,1)S(1)}, bf16[64,2048]{1,0:T(8,128)(2,1)S(1)}, u32[]{:S(2)}, u32[]{:S(2)}) collective-permute-start(bf16[64,2048]{1,0:T(8,128)(2,1)S(1)} %slice.99), channel_id=1, source_target_pairs={{0,8},{4,12},{8,0},{12,4},{1,9},{5,13},{9,1},{13,5},{2,10},{6,14},... | collective-permute-start | bytes 786440 | tf_op jit(solution)/shard_map/cond/branch_1_fun/ppermute | solution.py:211
  189.3 1.1 copy-start.9
  190.4 11.7 %collective-permute-start.15 = (bf16[128,2048]{1,0:T(8,128)(2,1)S(1)}, bf16[128,2048]{1,0:T(8,128)(2,1)S(1)}, u32[]{:S(2)}, u32[]{:S(2)}) collective-permute-start(bf16[128,2048]{1,0:T(8,128)(2,1)S(1)} %copy-done.9), channel_id=1, source_target_pairs={{0,8},{4,12},{8,0},{12,4},{1,9},{5,13},{9,1},{13,5},{2,10},{6,14},... | collective-permute-start | bytes 1572872 | tf_op jit(solution)/shard_map/ppermute | solution.py:211
  202.1 0.8 copy-start.12
